TPU v7x, 512 devices: a whole 4x8x8 slice. The times are simulated.
512 devices in a mesh: fsdp: 32 (over y, z_hi), tp: 16 (over x, z_lo, core).
Axes of the slice: x: 4, y: 8, z: 8 (z_hi: 4, z_lo: 2; z = z_hi * 2 + z_lo), core: 2. Of those that a mesh axis runs over, the one named last changes fastest.
Arguments:
- acts: bfloat16 [8192, 4096], P('fsdp'), may hold values from -6 to 6
- cots: bfloat16 [8192, 14336], P('fsdp', 'tp'), may hold values from -6 to 6
- weight: bfloat16 [4096, 14336], P('fsdp', 'tp'), may hold values from -0.09375 to 0.09375
- basis_in: bfloat16 [32, 128, 128], P('fsdp'), may hold values from -0.5 to 0.5
- basis_out: bfloat16 [16, 896, 896], P('tp', 'fsdp'), may hold values from -0.1875 to 0.1875
- eigen_in: float32 [4096], P('fsdp'), may hold values from 0.2 to 5
- eigen_out: float32 [14336], P('tp'), may hold values from 0.2 to 5
- forget_rows: int32 [2048], P('fsdp'), may hold values from 0 to 255
- retain_rows: int32 [1024], P('fsdp'), may hold values from 0 to 255
Outputs:
- retained: bfloat16 [1024, 14336], P('fsdp', 'tp')
- back_grads: bfloat16 [1024, 4096], P('fsdp')
All inputs are finite; a program needn't handle non-finite values.
Results may differ from a plain program's by a relative error of at most 0.022.
Values may be sent and summed in bfloat16 or wider, within the bound.
A program may use at most 64 MiB of HBM per device.

v0:
```python
import jax
import jax.numpy as jnp
from jax import lax
from jax.sharding import PartitionSpec as P

damping = 0.1
step_size = 0.5


def shards(acts, cots, weight, basis_in, basis_out, eigen_in, eigen_out, forget_rows, retain_rows):
    fsdp_count = lax.axis_size("fsdp")
    forget_local = forget_rows.shape[0]
    forget_count = forget_local * fsdp_count
    row_count = weight.shape[0]
    col_count = weight.shape[1]
    in_blocks = basis_in.shape[0]
    in_order = basis_in.shape[1]
    forget_acts = jnp.take(acts, forget_rows, axis=0)
    forget_cots = jnp.take(cots, forget_rows, axis=0)
    basis_full = lax.all_gather(basis_out, "fsdp", axis=1, tiled=True)
    out_blocks = basis_full.shape[0]
    out_order = basis_full.shape[2]
    rotated_cots = (
        jnp.einsum(
            "tgi,gij->tgj",
            forget_cots.reshape(forget_local, out_blocks, out_order),
            basis_full,
            preferred_element_type=jnp.float32,
        )
        .reshape(forget_local, col_count)
        .astype(jnp.bfloat16)
    )
    feature_cols = lax.all_to_all(forget_acts, "fsdp", split_axis=1, concat_axis=0, tiled=True)
    rotated_acts = (
        jnp.einsum(
            "tbi,bij->tbj",
            feature_cols.reshape(forget_count, in_blocks, in_order),
            basis_in,
            preferred_element_type=jnp.float32,
        )
        .reshape(forget_count, row_count)
        .astype(jnp.bfloat16)
    )
    moments = (
        lax.dot_general(
            rotated_acts,
            lax.all_gather(rotated_cots, "fsdp", axis=0, tiled=True),
            (((0,), (0,)), ((), ())),
            preferred_element_type=jnp.float32,
        )
        / forget_count
    )
    damped = eigen_in[:, None] * eigen_out[None, :] + damping
    scaled = (moments / damped).astype(jnp.bfloat16)
    back_out = (
        jnp.einsum(
            "dgi,gji->dgj",
            scaled.reshape(row_count, out_blocks, out_order),
            basis_full,
            preferred_element_type=jnp.float32,
        )
        .reshape(row_count, col_count)
        .astype(jnp.bfloat16)
    )
    update = jnp.einsum(
        "bij,bjc->bic",
        basis_in,
        back_out.reshape(in_blocks, in_order, col_count),
        preferred_element_type=jnp.float32,
    ).reshape(row_count, col_count)
    new_weight = (weight.astype(jnp.float32) + step_size * update).astype(jnp.bfloat16)
    retain_acts = jnp.take(acts, retain_rows, axis=0)
    retain_cots = jnp.take(cots, retain_rows, axis=0)
    retain_cols = lax.all_to_all(retain_acts, "fsdp", split_axis=1, concat_axis=0, tiled=True)
    retained = lax.psum_scatter(
        jnp.dot(retain_cols, new_weight, preferred_element_type=jnp.float32).astype(jnp.bfloat16),
        "fsdp",
        scatter_dimension=0,
        tiled=True,
    )
    grad_cols = lax.dot_general(
        lax.all_gather(retain_cots, "fsdp", axis=0, tiled=True),
        new_weight,
        (((1,), (1,)), ((), ())),
        preferred_element_type=jnp.float32,
    )
    grad_summed = lax.psum(grad_cols.astype(jnp.bfloat16), "tp")
    back_grads = lax.all_to_all(grad_summed, "fsdp", split_axis=0, concat_axis=1, tiled=True)
    return (retained, back_grads)


def solution(mesh):
    placed = (
        P("fsdp", None),
        P("fsdp", "tp"),
        P("fsdp", "tp"),
        P("fsdp", None, None),
        P("tp", "fsdp", None),
        P("fsdp"),
        P("tp"),
        P("fsdp"),
        P("fsdp"),
    )
    return jax.shard_map(
        shards,
        mesh=mesh,
        in_specs=placed,
        out_specs=(P("fsdp", "tp"), P("fsdp", None)),
        check_vma=False,
    )
```

profile of v0, /device:TPU:2, one launch (start us, length us, event | category | flops | bytes accessed | tf_op | source)
XLA Modules:
  0.0 666.9 jit_solution(1411980744719282719)
XLA Ops:
  7.2 1.7 copy.25
  9.0 0.7 compare_select_fusion
  9.7 1.9 gather_fusion.2
  11.5 0.7 compare_and_fusion
  12.2 99.0 %all-gather.4.cloned.1.call-done = bf16[1,896,896]{2,0,1:T(2,128)(2,1)} async-done(((bf16[1,28,896]{2,0,1:T(2,128)(2,1)}), bf16[1,896,896]{2,0,1:T(2,128)(2,1)}) %all-gather.4.cloned.1.call-update) | async-done | bytes 1605648 | tf_op jit(solution)/shard_map/all_gather | solution.py:20
  111.2 3.0 fusion.16
  114.9 0.7 broadcast_select_fusion
  115.7 0.9 gather_fusion.1
  116.6 1.1 bitcast_select_fusion
  117.6 6.8 %all-to-all-start.1 = ((bf16[64,32,128]{2,0,1:T(8,128)(2,1)}), bf16[64,32,128]{2,0,1:T(8,128)(2,1)S(1)}, u32[]{:S(2)}, u32[]{:S(2)}) async-start(bf16[64,32,128]{2,0,1:T(8,128)(2,1)} %bitcast_select_fusion), calls=%async_computation.1 | async-start | bytes 1048576 | tf_op jit(solution)/shard_map/all_to_all | solution.py:33
  124.5 0.7 gather_fusion
  125.4 0.8 bitcast_select_fusion.1
  126.2 16.7 %all-to-all-done.1 = bf16[64,32,128]{2,0,1:T(8,128)(2,1)S(1)} async-done(((bf16[64,32,128]{2,0,1:T(8,128)(2,1)}), bf16[64,32,128]{2,0,1:T(8,128)(2,1)S(1)}, u32[]{:S(2)}, u32[]{:S(2)}) %all-to-all-start.1) | async-done | bytes 524320 | tf_op jit(solution)/shard_map/all_to_all | solution.py:33
  142.9 5.6 all-to-all-start
  148.6 66.9 %all-gather.6.cloned.1.call-done = bf16[2048,896]{1,0:T(8,128)(2,1)} async-done(((bf16[64,896]{1,0:T(8,128)(2,1)}), bf16[2048,896]{1,0:T(8,128)(2,1)}) %all-gather.6.cloned.1.call-update) | async-done | bytes 3670032 | tf_op jit(solution)/shard_map/all_gather | solution.py:47
  215.6 3.0 fusion.13
  218.6 2.8 fusion.12
  221.4 78.9 %all-gather.8.cloned.1.call-done = bf16[1024,896]{1,0:T(8,128)(2,1)} async-done(((bf16[32,896]{1,0:T(8,128)(2,1)}), bf16[1024,896]{1,0:T(8,128)(2,1)}) %all-gather.8.cloned.1.call-update) | async-done | bytes 1835024 | tf_op jit(solution)/shard_map/all_gather | solution.py:82
  300.3 2.9 convolution_convert_fusion.2
  303.2 1.9 convolution_convert_fusion.1
  305.1 116.9 %all-reduce.2.cloned.1.call-done = bf16[32,32,128]{2,1,0:T(8,128)(2,1)} async-done(((bf16[32,32,128]{2,1,0:T(8,128)(2,1)}), bf16[32,32,128]{2,1,0:T(8,128)(2,1)}) %all-reduce.2.cloned.1.call-update) | async-done | bytes 262160 | tf_op jit(solution)/shard_map/psum | solution.py:87
  422.1 25.1 %all_to_all.48 = bf16[32,32,128]{2,1,0:T(8,128)(2,1)S(1)} all-to-all(bf16[32,32,128]{2,1,0:T(8,128)(2,1)} %all-reduce.2.cloned.1.call-done), channel_id=1, replica_groups=mesh['fsdp'=32,'tp'=16] {'fsdp'}, dimensions={0} | all-to-all | bytes 524288 | tf_op jit(solution)/shard_map/all_to_all | solution.py:88
  447.1 0.7 copy_bitcast_fusion
  447.8 212.5 %reduce-scatter.2.cloned.1.call-done = bf16[32,896]{1,0:T(8,128)(2,1)} async-done(((bf16[1024,896]{1,0:T(8,128)(2,1)}), bf16[32,896]{1,0:T(8,128)(2,1)}) %reduce-scatter.2.cloned.1.call-update) | async-done | bytes 57360 | tf_op jit(solution)/shard_map/reduce_scatter | solution.py:75
  (31 shorter events, 1.2 us)
Async XLA Ops:
  7.2 108.5 %copy-start = (bf16[256,4096]{1,0:T(8,128)(2,1)S(1)}, bf16[256,4096]{1,0:T(8,128)(2,1)}, u32[]{:S(2)}) copy-start(bf16[256,4096]{1,0:T(8,128)(2,1)} %param.9) | copy-start | bytes 6291460
  7.2 107.1 %copy-start.1 = (bf16[256,896]{1,0:T(8,128)(2,1)S(1)}, bf16[256,896]{1,0:T(8,128)(2,1)}, u32[]{:S(2)}) copy-start(bf16[256,896]{1,0:T(8,128)(2,1)} %param.10) | copy-start | bytes 1376260
  7.2 107.0 %copy-start.5 = (s32[32]{0:T(128)S(1)}, s32[32]{0:T(128)}, u32[]{:S(2)}) copy-start(s32[32]{0:T(128)} %param.17) | copy-start | bytes 388
  7.2 104.0 %all-gather.4.cloned.1.call-start = ((), (), s32[]{:S(2)}) async-start(), calls=%async_computation.4 | async-start | bytes 3311616 | tf_op jit(solution)/shard_map/all_gather | solution.py:20
  9.0 206.6 %all-gather.6.cloned.1.call-start = ((), (), s32[]{:S(2)}) async-start(), calls=%async_computation.5 | async-start | bytes 3784704 | tf_op jit(solution)/shard_map/all_gather | solution.py:47
  114.2 186.1 %all-gather.8.cloned.1.call-start = ((), (), s32[]{:S(2)}) async-start(), calls=%async_computation.7 | async-start | bytes 1892352 | tf_op jit(solution)/shard_map/all_gather | solution.py:82
  116.5 8.7 %copy-start.2 = (bf16[128,896]{1,0:T(8,128)(2,1)S(1)}, bf16[128,896]{1,0:T(8,128)(2,1)}, u32[]{:S(2)}) copy-start(bf16[128,896]{1,0:T(8,128)(2,1)} %param.11) | copy-start | bytes 688132
  117.6 25.3 %all-to-all-start.1 = ((bf16[64,32,128]{2,0,1:T(8,128)(2,1)}), bf16[64,32,128]{2,0,1:T(8,128)(2,1)S(1)}, u32[]{:S(2)}, u32[]{:S(2)}) async-start(bf16[64,32,128]{2,0,1:T(8,128)(2,1)} %bitcast_select_fusion), calls=%async_computation.1 | async-start | bytes 1048576 | tf_op jit(solution)/shard_map/all_to_all | solution.py:33
  124.4 91.1 %copy-start.3 = (bf16[1,128,128]{2,1,0:T(8,128)(2,1)S(1)}, bf16[1,128,128]{2,1,0:T(8,128)(2,1)}, u32[]{:S(2)}) copy-start(bf16[1,128,128]{2,1,0:T(8,128)(2,1)} %param.12) | copy-start | bytes 98308
  124.5 91.1 %copy-start.4 = (f32[896]{0:T(1024)S(1)}, f32[896]{0:T(1024)}, u32[]{:S(2)}) copy-start(f32[896]{0:T(1024)} %param.15) | copy-start | bytes 10756
  124.5 91.1 %copy-start.6 = (f32[128]{0:T(128)S(1)}, f32[128]{0:T(128)}, u32[]{:S(2)}) copy-start(f32[128]{0:T(128)} %param.14) | copy-start | bytes 1540
  142.9 160.3 %all-to-all-start = ((bf16[32,32,128]{2,0,1:T(8,128)(2,1)}), bf16[32,32,128]{2,0,1:T(8,128)(2,1)S(1)}, u32[]{:S(2)}, u32[]{:S(2)}) async-start(bf16[32,32,128]{2,0,1:T(8,128)(2,1)} %bitcast_select_fusion.1), calls=%async_computation | async-start | bytes 524288 | tf_op jit(solution)/shard_map/all_to_all | solution.py:74
  148.6 273.5 %all-reduce.2.cloned.1.call-start = ((), (), s32[]{:S(2)}) async-start(), calls=%async_computation.8 | async-start | bytes 524288 | tf_op jit(solution)/shard_map/psum | solution.py:87
  303.2 357.2 %reduce-scatter.2.cloned.1.call-start = ((), (), s32[]{:S(2)}) async-start(), calls=%async_computation.6 | async-start | bytes 1892352 | tf_op jit(solution)/shard_map/reduce_scatter | solution.py:75
Sparse Core Ops, SparseCore 0:
  11.7 99.4 all-gather.3
  114.4 101.1 all-gather.5
  219.3 80.9 all-gather.7
  303.3 118.7 all-reduce.1
  427.6 232.6 reduce-scatter.1
where the time goes:
time: 667 us
  waiting for transfers between devices  591 us (89%)
  blocking collectives  25.1 us (4%)
  between operations  14 us (2%)
  matrix products  13.6 us (2%)
  starting transfers between devices  12.7 us (2%)
  local copies, waits for them, and re-layouts  6.69 us (1%)
    reduce_scatter x1, waiting for transfers between devices, shards(): lax.psum_scatter(jnp.dot(retain_cols, new_weight, preferred_element_type=...  213 us
    psum x1, waiting for transfers between devices, shards(): grad_summed = lax.psum(grad_cols.astype(jnp.bfloat16), 'tp')  117 us
    all_gather x1, waiting for transfers between devices, shards(): basis_full = lax.all_gather(basis_out, 'fsdp', axis=1, tiled=True)  99 us
    all_gather x1, waiting for transfers between devices, shards(): lax.all_gather(retain_cots, 'fsdp', axis=0, tiled=True)  78.9 us
    all_gather x1, waiting for transfers between devices, shards(): lax.all_gather(rotated_cots, 'fsdp', axis=0, tiled=True)  66.9 us
    all_to_all x1, blocking collectives, shards(): lax.all_to_all(grad_summed, 'fsdp', split_axis=0, concat_axis=1, tiled=True)  25.1 us
    all_to_all x1, waiting for transfers between devices, shards(): lax.all_to_all(forget_acts, 'fsdp', split_axis=1, concat_axis=0, tiled=True)  16.7 us
  transfers between devices with their start and end apart: 7, of which 6 were waited for; matrix products, arithmetic and copies ran while one was open for 3% of the time, Pallas kernels for 0%

commit v1 on v0

--- a/solution.py
+++ b/solution.py
@@ -84,7 +84,7 @@
         (((1,), (1,)), ((), ())),
         preferred_element_type=jnp.float32,
     )
-    grad_summed = lax.psum(grad_cols.astype(jnp.bfloat16), "tp")
+    grad_summed = jnp.sum(lax.all_gather(grad_cols.astype(jnp.bfloat16), "tp"), axis=0)
     back_grads = lax.all_to_all(grad_summed, "fsdp", split_axis=0, concat_axis=1, tiled=True)
     return (retained, back_grads)
 

time: 667 us -> 583 us (0.87)
  waiting for transfers between devices: 591 us -> 491 us
  blocking collectives: 25.1 us -> 44.2 us
    psum x1 -> x0, waiting for transfers between devices: 117 us -> none  [shards(): grad_summed = lax.psum(grad_cols.astype(jnp.bfloat16), 'tp')]
    all_to_all x0 -> x1, blocking collectives: none -> 20.2 us  [shards(): lax.all_to_all(retain_acts, 'fsdp', split_axis=1, concat_axis=0, tiled=True)]
    all_gather x0 -> x1, waiting for transfers between devices: none -> 18.8 us  [shards(): lax.all_gather(grad_cols.astype(jnp.bfloat16), 'tp')]
    reduce_scatter x1, waiting for transfers between devices: 213 us -> 204 us  [shards(): lax.psum_scatter(jnp.dot(retain_cols, new_weight, preferred_element_type=...]
  transfers between devices with their start and end apart: 7 -> 6, of which waited for: 6 -> 6; matrix products, arithmetic and copies ran while one was open for 3% -> 3% of each run, Pallas kernels for 0% -> 0%
where the time goes in v1:
time: 583 us; the launch traced here: 582 us
  waiting for transfers between devices  491 us (84%)
  blocking collectives  44.2 us (8%)
  between operations  13.9 us (2%)
  matrix products  13.6 us (2%)
  starting transfers between devices  7.03 us (1%)
  local copies, waits for them, and re-layouts  6.69 us (1%)
  other arithmetic  6.08 us (1%)
    reduce_scatter x1, waiting for transfers between devices, shards(): lax.psum_scatter(jnp.dot(retain_cols, new_weight, preferred_element_type=...  204 us
    all_gather x1, waiting for transfers between devices, shards(): basis_full = lax.all_gather(basis_out, 'fsdp', axis=1, tiled=True)  99 us
    all_gather x1, waiting for transfers between devices, shards(): lax.all_gather(retain_cots, 'fsdp', axis=0, tiled=True)  78.9 us
    all_gather x1, waiting for transfers between devices, shards(): lax.all_gather(rotated_cots, 'fsdp', axis=0, tiled=True)  71.6 us
    all_to_all x1, blocking collectives, shards(): lax.all_to_all(grad_summed, 'fsdp', split_axis=0, concat_axis=1, tiled=True)  24 us
    all_to_all x1, blocking collectives, shards(): lax.all_to_all(retain_acts, 'fsdp', split_axis=1, concat_axis=0, tiled=True)  20.2 us
    all_gather x1, waiting for transfers between devices, shards(): lax.all_gather(grad_cols.astype(jnp.bfloat16), 'tp')  18.8 us
    all_to_all x1, waiting for transfers between devices, shards(): lax.all_to_all(forget_acts, 'fsdp', split_axis=1, concat_axis=0, tiled=True)  18.3 us
  transfers between devices with their start and end apart: 6, of which 6 were waited for; matrix products, arithmetic and copies ran while one was open for 3% of the time, Pallas kernels for 0%

profile of v1, /device:TPU:2, one launch (start us, length us, event | category | flops | bytes accessed | tf_op | source)
XLA Modules:
  0.0 582.0 jit_solution(3757615406161461350)
XLA Ops:
  7.2 1.7 copy.27
  9.0 0.7 compare_select_fusion
  9.7 1.9 gather_fusion.2
  11.5 0.7 compare_and_fusion
  12.2 99.0 %all-gather.6.cloned.1.call-done = bf16[1,896,896]{2,0,1:T(2,128)(2,1)} async-done(((bf16[1,28,896]{2,0,1:T(2,128)(2,1)}), bf16[1,896,896]{2,0,1:T(2,128)(2,1)}) %all-gather.6.cloned.1.call-update) | async-done | bytes 1605648 | tf_op jit(solution)/shard_map/all_gather | solution.py:20
  111.2 3.0 fusion.16
  114.9 0.7 broadcast_select_fusion
  115.7 0.9 gather_fusion.1
  116.6 1.0 bitcast_select_fusion
  117.6 6.8 %all-to-all-start.1 = ((bf16[64,32,128]{2,0,1:T(8,128)(2,1)}), bf16[64,32,128]{2,0,1:T(8,128)(2,1)S(1)}, u32[]{:S(2)}, u32[]{:S(2)}) async-start(bf16[64,32,128]{2,0,1:T(8,128)(2,1)} %bitcast_select_fusion), calls=%async_computation.1 | async-start | bytes 1048576 | tf_op jit(solution)/shard_map/all_to_all | solution.py:33
  124.7 18.3 %all-to-all-done.1 = bf16[64,32,128]{2,0,1:T(8,128)(2,1)S(1)} async-done(((bf16[64,32,128]{2,0,1:T(8,128)(2,1)}), bf16[64,32,128]{2,0,1:T(8,128)(2,1)S(1)}, u32[]{:S(2)}, u32[]{:S(2)}) %all-to-all-start.1) | async-done | bytes 524320 | tf_op jit(solution)/shard_map/all_to_all | solution.py:33
  143.0 71.6 %all-gather.8.cloned.1.call-done = bf16[2048,896]{1,0:T(8,128)(2,1)} async-done(((bf16[64,896]{1,0:T(8,128)(2,1)}), bf16[2048,896]{1,0:T(8,128)(2,1)}) %all-gather.8.cloned.1.call-update) | async-done | bytes 3670032 | tf_op jit(solution)/shard_map/all_gather | solution.py:47
  214.5 3.0 fusion.13
  217.6 2.8 fusion.12
  220.4 78.9 %all-gather.10.cloned.1.call-done = bf16[1024,896]{1,0:T(8,128)(2,1)} async-done(((bf16[32,896]{1,0:T(8,128)(2,1)}), bf16[1024,896]{1,0:T(8,128)(2,1)}) %all-gather.10.cloned.1.call-update) | async-done | bytes 1835024 | tf_op jit(solution)/shard_map/all_gather | solution.py:82
  299.3 2.8 convolution_convert_fusion.2
  302.2 0.7 gather_fusion
  303.0 20.2 %all_to_all.48 = bf16[32,32,128]{2,0,1:T(8,128)(2,1)S(1)} all-to-all(bf16[32,32,128]{2,0,1:T(8,128)(2,1)S(1)} %bitcast_select_fusion.1), channel_id=1, replica_groups=mesh['fsdp'=32,'tp'=16] {'fsdp'}, dimensions={1} | all-to-all | bytes 524288 | tf_op jit(solution)/shard_map/all_to_all | solution.py:74
  323.2 1.9 convolution_convert_fusion.1
  325.1 18.8 %all-gather.12.cloned.1.call-done = bf16[16384,128]{1,0:T(8,128)(2,1)} async-done(((bf16[1024,128]{1,0:T(8,128)(2,1)}), bf16[16384,128]{1,0:T(8,128)(2,1)}) %all-gather.12.cloned.1.call-update) | async-done | bytes 4194320 | tf_op jit(solution)/shard_map/all_gather | solution.py:87
  343.9 2.9 reduce_sum.12
  346.8 24.0 %all_to_all.49 = bf16[32,32,128]{2,1,0:T(8,128)(2,1)S(1)} all-to-all(bf16[32,32,128]{2,1,0:T(8,128)(2,1)S(1)} %bitcast.64), channel_id=1, replica_groups=mesh['fsdp'=32,'tp'=16] {'fsdp'}, dimensions={0} | all-to-all | bytes 524288 | tf_op jit(solution)/shard_map/all_to_all | solution.py:88
  370.8 0.7 copy_bitcast_fusion
  371.5 204.0 %reduce-scatter.2.cloned.1.call-done = bf16[32,896]{1,0:T(8,128)(2,1)} async-done(((bf16[1024,896]{1,0:T(8,128)(2,1)}), bf16[32,896]{1,0:T(8,128)(2,1)}) %reduce-scatter.2.cloned.1.call-update) | async-done | bytes 57360 | tf_op jit(solution)/shard_map/reduce_scatter | solution.py:75
  (31 shorter events, 1.3 us)
Async XLA Ops:
  7.2 108.5 %copy-start = (bf16[256,4096]{1,0:T(8,128)(2,1)S(1)}, bf16[256,4096]{1,0:T(8,128)(2,1)}, u32[]{:S(2)}) copy-start(bf16[256,4096]{1,0:T(8,128)(2,1)} %param.9) | copy-start | bytes 6291460
  7.2 107.1 %copy-start.1 = (bf16[256,896]{1,0:T(8,128)(2,1)S(1)}, bf16[256,896]{1,0:T(8,128)(2,1)}, u32[]{:S(2)}) copy-start(bf16[256,896]{1,0:T(8,128)(2,1)} %param.10) | copy-start | bytes 1376260
  7.2 107.0 %copy-start.5 = (s32[32]{0:T(128)S(1)}, s32[32]{0:T(128)}, u32[]{:S(2)}) copy-start(s32[32]{0:T(128)} %param.17) | copy-start | bytes 388
  7.2 104.0 %all-gather.6.cloned.1.call-start = ((), (), s32[]{:S(2)}) async-start(), calls=%async_computation.4 | async-start | bytes 3311616 | tf_op jit(solution)/shard_map/all_gather | solution.py:20
  9.0 205.6 %all-gather.8.cloned.1.call-start = ((), (), s32[]{:S(2)}) async-start(), calls=%async_computation.5 | async-start | bytes 3784704 | tf_op jit(solution)/shard_map/all_gather | solution.py:47
  114.2 185.1 %all-gather.10.cloned.1.call-start = ((), (), s32[]{:S(2)}) async-start(), calls=%async_computation.7 | async-start | bytes 1892352 | tf_op jit(solution)/shard_map/all_gather | solution.py:82
  116.5 8.0 %copy-start.2 = (bf16[128,896]{1,0:T(8,128)(2,1)S(1)}, bf16[128,896]{1,0:T(8,128)(2,1)}, u32[]{:S(2)}) copy-start(bf16[128,896]{1,0:T(8,128)(2,1)} %param.11) | copy-start | bytes 688132
  116.6 98.0 %copy-start.3 = (bf16[1,128,128]{2,1,0:T(8,128)(2,1)S(1)}, bf16[1,128,128]{2,1,0:T(8,128)(2,1)}, u32[]{:S(2)}) copy-start(bf16[1,128,128]{2,1,0:T(8,128)(2,1)} %param.12) | copy-start | bytes 98308
  116.6 98.0 %copy-start.4 = (f32[896]{0:T(1024)S(1)}, f32[896]{0:T(1024)}, u32[]{:S(2)}) copy-start(f32[896]{0:T(1024)} %param.15) | copy-start | bytes 10756
  116.6 98.0 %copy-start.6 = (f32[128]{0:T(128)S(1)}, f32[128]{0:T(128)}, u32[]{:S(2)}) copy-start(f32[128]{0:T(128)} %param.14) | copy-start | bytes 1540
  117.6 25.3 %all-to-all-start.1 = ((bf16[64,32,128]{2,0,1:T(8,128)(2,1)}), bf16[64,32,128]{2,0,1:T(8,128)(2,1)S(1)}, u32[]{:S(2)}, u32[]{:S(2)}) async-start(bf16[64,32,128]{2,0,1:T(8,128)(2,1)} %bitcast_select_fusion), calls=%async_computation.1 | async-start | bytes 1048576 | tf_op jit(solution)/shard_map/all_to_all | solution.py:33
  124.5 219.4 %all-gather.12.cloned.1.call-start = ((), (), s32[]{:S(2)}) async-start(), calls=%async_computation.8 | async-start | bytes 4456448 | tf_op jit(solution)/shard_map/all_gather | solution.py:87
  302.1 273.4 %reduce-scatter.2.cloned.1.call-start = ((), (), s32[]{:S(2)}) async-start(), calls=%async_computation.6 | async-start | bytes 1892352 | tf_op jit(solution)/shard_map/reduce_scatter | solution.py:75
Sparse Core Ops, SparseCore 0:
  11.7 99.4 all-gather.5
  114.9 99.5 all-gather.7
  218.3 80.9 all-gather.9
  302.3 41.5 all-gather.11
  348.8 226.6 reduce-scatter.1
